TPU v7x, 256 devices: a whole 4x4x8 slice. The times are simulated.
256 devices in a mesh: tm: 8 (over z), chan: 32 (over x, y, core).
Axes of the slice: x: 4, y: 4, z: 8, core: 2. Of those that a mesh axis runs over, the one named last changes fastest.
Arguments:
- traces: bfloat16 [8192, 32768], P('chan', 'tm'), may hold values from -80 to 80
- band_edges: int32 [32, 2], P('tm'), may hold values from 0 to 256, as said below
- slot_pairs: int32 [320, 2], P('chan'), may hold values from -1 to 63, as said below
Outputs:
- cross_spectra: float32 [320, 32, 2, 128, 128], P('chan', 'tm')
Inputs may be any that keep to these rules, and one draw needn't show every extreme that they name: `band_edges`: row k holds the first bin and one past the last bin of band k; the bands tile the bins 0 to 255 in order, each one bin wide or more, and the bands k * 4 to (k + 1) * 4 - 1 cover exactly the bins k * 32 to (k + 1) * 32 - 1. `slot_pairs`: row r = o * 5 + s belongs to block o; it holds a pair (a, b) with a <= b <= a + 2 and o equal to a or to b, or (-1, -1) for an empty row. No pair appears twice. In every draw some block fills all 5 of its rows; the other blocks own uneven numbers of pairs, in rows of any order.
All inputs are finite; a program needn't handle non-finite values.
Results may differ from a plain program's by a relative error of at most 0.0037.
Values may be sent and summed in bfloat16 or wider, within the bound.
A program may use at most 128 MiB of HBM per device.

v0:
```python
import math

import jax
import jax.numpy as jnp
import numpy as np
from jax import lax
from jax.sharding import PartitionSpec as P

CB = 128
SEG = 512
NF = 256
SMOOTH = 64
REACH = 2
BLK_DEV = 2


whiten_eps = 1e-06


def shifted(array, axis, by):
    count = lax.axis_size(axis)
    pairs = [(i, i + by) for i in range(count) if 0 <= i + by < count]
    return lax.ppermute(array, axis, pairs)


def extended_2(cells, sides, width):
    for axis, dim in sides:
        count = lax.axis_size(axis)
        ends = count - 1
        head = lax.slice_in_dim(cells, 0, width, axis=dim)
        tail = lax.slice_in_dim(cells, cells.shape[dim] - width, cells.shape[dim], axis=dim)
        cells = jnp.concatenate(
            [
                lax.ppermute(tail, axis, [(i, (i + 1) % count) for i in range(ends)]),
                cells,
                lax.ppermute(head, axis, [((i + 1) % count, i) for i in range(ends)]),
            ],
            axis=dim,
        )
    return cells


def transform_tables(seg_len, bin_count):
    sample_ids = jnp.arange(seg_len, dtype=jnp.int32)[:, None]
    bin_ids = jnp.arange(bin_count, dtype=jnp.int32)[None, :]
    phases = (sample_ids * bin_ids % seg_len).astype(jnp.float32) * (2.0 * math.pi / seg_len)
    hann_taper = 0.5 - 0.5 * jnp.cos(
        jnp.arange(seg_len, dtype=jnp.float32) * (2.0 * math.pi / seg_len)
    )
    cosine = hann_taper[:, None] * jnp.cos(phases)
    sine_part = -hann_taper[:, None] * jnp.sin(phases)
    return jnp.stack([cosine, sine_part]).astype(jnp.bfloat16)


def window_mean(power, axis, bin_count, half_width):
    totals = jnp.cumsum(power, axis=axis)
    front_shape = list(power.shape)
    front_shape[axis] = half_width + 1
    front = jnp.zeros(tuple(front_shape), power.dtype)
    last_total = lax.slice_in_dim(totals, bin_count - 1, bin_count, axis=axis)
    back_shape = list(power.shape)
    back_shape[axis] = half_width
    back = jnp.broadcast_to(last_total, tuple(back_shape))
    extended = jnp.concatenate([front, totals, back], axis=axis)
    upper_part = lax.slice_in_dim(
        extended, 2 * half_width + 1, 2 * half_width + 1 + bin_count, axis=axis
    )
    lower_part = lax.slice_in_dim(extended, 0, bin_count, axis=axis)
    bin_ids = np.arange(bin_count)
    window_count = (
        np.minimum(bin_ids + half_width + 1, bin_count) - np.maximum(bin_ids - half_width, 0)
    ).astype(np.float32)
    count_shape = [1] * power.ndim
    count_shape[axis] = bin_count
    counts = jnp.asarray(window_count.reshape(count_shape), power.dtype)
    return (upper_part - lower_part) / counts


def band_weights(band_edges, bin_ids, segment_count):
    lower_edge = band_edges[:, 0:1]
    upper_edge = band_edges[:, 1:2]
    inside = ((bin_ids[None, :] >= lower_edge) & (bin_ids[None, :] < upper_edge)).astype(
        jnp.float32
    )
    band_width = (upper_edge - lower_edge).astype(jnp.float32)
    return inside / jnp.sqrt(segment_count * band_width)


def pair_cross(left_side, right_side, weights):
    swapped = jnp.stack([left_side[1], -left_side[0]])
    real_part = jnp.einsum(
        "psfi,psfj->fij", left_side, right_side, preferred_element_type=jnp.float32
    )
    imag_part = jnp.einsum(
        "psfi,psfj->fij", swapped, right_side, preferred_element_type=jnp.float32
    )
    stacked = jnp.stack([real_part, imag_part])
    return jnp.einsum("kf,qfij->kqij", weights, stacked, precision=lax.Precision.HIGHEST)


def shards(traces, band_edges, slot_pairs):
    channel_rows, local_samples = traces.shape
    half_seg = SEG // 2
    local_segments = local_samples // half_seg
    leading = traces[:, :half_seg]
    following = shifted(leading, "tm", -1)
    extended = jnp.concatenate([traces, following], axis=1)
    halves = extended.reshape(channel_rows, local_segments + 1, half_seg)
    frames = jnp.concatenate([halves[:, :-1], halves[:, 1:]], axis=2)
    frames = frames.reshape(BLK_DEV, CB, local_segments, SEG)
    tables = transform_tables(SEG, NF)
    spectra = jnp.einsum("bcsn,pnf->bpsfc", frames, tables, preferred_element_type=jnp.float32)
    spectral_power = spectra[:, 0] * spectra[:, 0] + spectra[:, 1] * spectra[:, 1]
    smooth = window_mean(spectral_power, 2, NF, SMOOTH)
    whitened = (spectra * lax.rsqrt(smooth + whiten_eps)[:, None]).astype(jnp.bfloat16)
    grouped = lax.all_to_all(whitened, "tm", split_axis=3, concat_axis=2, tiled=True)
    segment_count = grouped.shape[2]
    run_bins = grouped.shape[3]
    bin_ids = band_edges[0, 0] + jnp.arange(run_bins, dtype=jnp.int32)
    weights = band_weights(band_edges, bin_ids, segment_count)
    own_first = lax.axis_index("chan") * BLK_DEV
    window = extended_2(grouped, (("chan", 0),), REACH)
    window_first = own_first - REACH
    window_last = window.shape[0] - 1

    def owner_slot(slot_pair):
        first_index = jnp.clip(slot_pair[0] - window_first, 0, window_last)
        second_index = jnp.clip(slot_pair[1] - window_first, 0, window_last)
        left_side = lax.dynamic_index_in_dim(window, first_index, 0, keepdims=False)
        right_side = lax.dynamic_index_in_dim(window, second_index, 0, keepdims=False)
        result = pair_cross(left_side, right_side, weights)
        return jnp.where(slot_pair[0] >= 0, result, jnp.zeros_like(result))

    cross_spectra = lax.map(owner_slot, slot_pairs)
    return cross_spectra


def solution(mesh):
    in_specs = (P("chan", "tm"), P("tm", None), P("chan", None))
    out_specs = P("chan", "tm", None, None, None)
    return jax.shard_map(shards, mesh=mesh, in_specs=in_specs, out_specs=out_specs, check_vma=False)
```

profile of v0, /device:TPU:25, one launch (start us, length us, event | category | flops | bytes accessed | tf_op | source)
XLA Modules:
  0.0 482.0 jit_solution(10701524008742664351)
XLA Ops:
  13.0 7.9 %copy.45 = bf16[256,16,512]{2,1,0:T(8,128)(2,1)} copy(bf16[256,16,512]{0,2,1:T(8,128)(2,1)} %pad_maximum_fusion.3) | data formatting | bytes 8388608 | tf_op jit(solution)/shard_map/concatenate | solution.py:109
  20.9 9.0 %fusion.51 = f32[2,2,16,256,128]{4,3,2,0,1:T(8,128)S(1)} fusion(bf16[2,128,16,512]{3,2,1,0:T(8,128)(2,1)} %bitcast.97, bf16[1,512,256]{1,2,0:T(8,128)(2,1)S(1)} %get-tuple-element.117, bf16[1,512,256]{1,2,0:T(8,128)(2,1)S(1)} %get-tuple-element.118), kind=kOutput, calls=%fused_computation.53 | convolution fusion | flops 2148532224 | bytes 13107200 | tf_op jit(solution)/shard_map/bcsn,pnf->bpsfc/dot_general | solution.py:112
  38.3 5.4 %multiply_convert_fusion = bf16[2,2,16,256,128]{4,3,2,0,1:T(8,128)(2,1)} fusion(f32[2,2,16,256,128]{4,3,2,0,1:T(8,128)S(1)} %fusion.51, f32[2,16,256,128]{3,2,1,0:T(8,128)} %fusion.44), kind=kLoop, calls=%fused_computation.36 | loop fusion | flops 4194304 | bytes 16777216 | tf_op jit(solution)/shard_map/convert_element_type | solution.py:115
  43.7 4.9 %copy.49 = bf16[2,2,16,256,128]{4,2,0,1,3:T(8,128)(2,1)S(1)} copy(bf16[2,2,16,256,128]{4,3,2,0,1:T(8,128)(2,1)} %multiply_convert_fusion) | data formatting | bytes 8388608 | tf_op jit(solution)/shard_map/convert_element_type | solution.py:115
  48.6 101.0 %all_to_all.18 = bf16[2,2,16,256,128]{4,2,0,1,3:T(8,128)(2,1)S(1)} all-to-all(bf16[2,2,16,256,128]{4,2,0,1,3:T(8,128)(2,1)S(1)} %copy.49), channel_id=1, replica_groups=mesh['tm'=8,'chan'=32] {'tm'}, dimensions={3} | all-to-all | bytes 8388608 | tf_op jit(solution)/shard_map/all_to_all | solution.py:116
  149.6 6.8 %copy.51 = bf16[2,2,8,16,32,128]{5,4,3,2,1,0:T(8,128)(2,1)} copy(bf16[2,2,8,16,32,128]{5,3,0,1,4,2:T(8,128)(2,1)S(1)} %bitcast.103) | data formatting | bytes 8388608 | tf_op jit(solution)/shard_map/all_to_all | solution.py:116
  156.4 6.3 %collective-permute-start.1 = (bf16[2,2,128,32,128]{4,3,2,1,0:T(8,128)(2,1)}, bf16[2,2,128,32,128]{4,3,2,1,0:T(8,128)(2,1)}, u32[]{:S(2)}, u32[]{:S(2)}) collective-permute-start(bf16[2,2,128,32,128]{4,3,2,1,0:T(8,128)(2,1)} %bitcast.16), channel_id=1, source_target_pairs={{0,1},{1,2},{2,3},{3,4},{4,5},{5,6},{6,7},{7,8},{8,9},{9,10},{10,1... | collective-permute-start | bytes 12582920 | tf_op jit(solution)/shard_map/ppermute | solution.py:34
  165.8 42.7 %collective-permute-done.1 = bf16[2,2,128,32,128]{4,3,2,1,0:T(8,128)(2,1)} collective-permute-done((bf16[2,2,128,32,128]{4,3,2,1,0:T(8,128)(2,1)}, bf16[2,2,128,32,128]{4,3,2,1,0:T(8,128)(2,1)}, u32[]{:S(2)}, u32[]{:S(2)}) %collective-permute-start.1) | collective-permute-done | bytes 4194336 | tf_op jit(solution)/shard_map/ppermute | solution.py:34
  208.5 6.5 %collective-permute-done.2 = bf16[2,2,128,32,128]{4,3,2,1,0:T(8,128)(2,1)} collective-permute-done((bf16[2,2,128,32,128]{4,3,2,1,0:T(8,128)(2,1)}, bf16[2,2,128,32,128]{4,3,2,1,0:T(8,128)(2,1)}, u32[]{:S(2)}, u32[]{:S(2)}) %collective-permute-start.2) | collective-permute-done | bytes 4194336 | tf_op jit(solution)/shard_map/ppermute | solution.py:36
  215.0 10.5 %pad_maximum_fusion.1 = bf16[6,2,128,32,128]{4,3,2,1,0:T(8,128)(2,1)} fusion(bf16[2,2,128,32,128]{4,3,2,1,0:T(8,128)(2,1)} %collective-permute-done.2, bf16[2,2,128,32,128]{4,3,2,1,0:T(8,128)(2,1)} %bitcast.16, bf16[2,2,128,32,128]{4,3,2,1,0:T(8,128)(2,1)} %collective-permute-done.1), kind=kLoop, calls=%fused_computation.35 | loop fusion | flops 12582912 | bytes 25165824 | tf_op jit(solution)/shard_map/concatenate | solution.py:32
  225.5 17.9 %copy.52 = bf16[6,2,128,32,128]{2,4,3,1,0:T(8,128)(2,1)} copy(bf16[6,2,128,32,128]{4,3,2,1,0:T(8,128)(2,1)} %pad_maximum_fusion.1) | data formatting | bytes 25165824
  243.4 238.6 %while.11 = (s32[]{:T(128)}, f32[10,4,2,128,128]{4,3,2,1,0:T(8,128)}, s32[10,2]{0,1:T(2,128)S(1)}, s32[]{:T(128)}, bf16[6,2,128,32,128]{2,4,3,1,0:T(8,128)(2,1)}...) while((s32[]{:T(128)}, ...), condition=%wide.region_3.4_spmd.clone, body=%wide.region_2.3_spmd.clone.sunk | while | flops 589955712 | bytes 51905496 | solution.py:134
  245.1 4.7 constant_dynamic-slice_fusion.6
  259.9 6.6 %fusion.86 = f32[1,4,2,128,128]{4,1,3,2,0:T(4,128)S(1)} fusion(f32[2,32,128,128]{3,2,1,0:T(8,128)} %pad_maximum_fusion.6, pred[]{:T(512)S(6)} %ge.54, f32[4]{0:T(128)S(1)} %get-tuple-element.220, s32[32]{0:T(128)S(1)} %get-tuple-element.219, s32[4]{0:T(128)S(1)} %get-tuple-element.218, s32[4]{0:T(128)S(1)} %get-tuple-element.217), kind=kOutput, calls=%fused_computation.16.clone.1 | convolution fusion | flops 50463360 | bytes 4718769 | tf_op jit(solution)/shard_map/while/body/eval_jaxpr/kf,qfij->kqij/dot_general | solution.py:98
  268.9 4.7 constant_dynamic-slice_fusion.6
  283.7 6.6 %fusion.86 = f32[1,4,2,128,128]{4,1,3,2,0:T(4,128)S(1)} fusion(f32[2,32,128,128]{3,2,1,0:T(8,128)} %pad_maximum_fusion.6, pred[]{:T(512)S(6)} %ge.54, f32[4]{0:T(128)S(1)} %get-tuple-element.220, s32[32]{0:T(128)S(1)} %get-tuple-element.219, s32[4]{0:T(128)S(1)} %get-tuple-element.218, s32[4]{0:T(128)S(1)} %get-tuple-element.217), kind=kOutput, calls=%fused_computation.16.clone.1 | convolution fusion | flops 50463360 | bytes 4718769 | tf_op jit(solution)/shard_map/while/body/eval_jaxpr/kf,qfij->kqij/dot_general | solution.py:98
  307.6 6.6 %fusion.86 = f32[1,4,2,128,128]{4,1,3,2,0:T(4,128)S(1)} fusion(f32[2,32,128,128]{3,2,1,0:T(8,128)} %pad_maximum_fusion.6, pred[]{:T(512)S(6)} %ge.54, f32[4]{0:T(128)S(1)} %get-tuple-element.220, s32[32]{0:T(128)S(1)} %get-tuple-element.219, s32[4]{0:T(128)S(1)} %get-tuple-element.218, s32[4]{0:T(128)S(1)} %get-tuple-element.217), kind=kOutput, calls=%fused_computation.16.clone.1 | convolution fusion | flops 50463360 | bytes 4718769 | tf_op jit(solution)/shard_map/while/body/eval_jaxpr/kf,qfij->kqij/dot_general | solution.py:98
  331.5 6.6 %fusion.86 = f32[1,4,2,128,128]{4,1,3,2,0:T(4,128)S(1)} fusion(f32[2,32,128,128]{3,2,1,0:T(8,128)} %pad_maximum_fusion.6, pred[]{:T(512)S(6)} %ge.54, f32[4]{0:T(128)S(1)} %get-tuple-element.220, s32[32]{0:T(128)S(1)} %get-tuple-element.219, s32[4]{0:T(128)S(1)} %get-tuple-element.218, s32[4]{0:T(128)S(1)} %get-tuple-element.217), kind=kOutput, calls=%fused_computation.16.clone.1 | convolution fusion | flops 50463360 | bytes 4718769 | tf_op jit(solution)/shard_map/while/body/eval_jaxpr/kf,qfij->kqij/dot_general | solution.py:98
  355.3 6.6 %fusion.86 = f32[1,4,2,128,128]{4,1,3,2,0:T(4,128)S(1)} fusion(f32[2,32,128,128]{3,2,1,0:T(8,128)} %pad_maximum_fusion.6, pred[]{:T(512)S(6)} %ge.54, f32[4]{0:T(128)S(1)} %get-tuple-element.220, s32[32]{0:T(128)S(1)} %get-tuple-element.219, s32[4]{0:T(128)S(1)} %get-tuple-element.218, s32[4]{0:T(128)S(1)} %get-tuple-element.217), kind=kOutput, calls=%fused_computation.16.clone.1 | convolution fusion | flops 50463360 | bytes 4718769 | tf_op jit(solution)/shard_map/while/body/eval_jaxpr/kf,qfij->kqij/dot_general | solution.py:98
  379.2 6.6 %fusion.86 = f32[1,4,2,128,128]{4,1,3,2,0:T(4,128)S(1)} fusion(f32[2,32,128,128]{3,2,1,0:T(8,128)} %pad_maximum_fusion.6, pred[]{:T(512)S(6)} %ge.54, f32[4]{0:T(128)S(1)} %get-tuple-element.220, s32[32]{0:T(128)S(1)} %get-tuple-element.219, s32[4]{0:T(128)S(1)} %get-tuple-element.218, s32[4]{0:T(128)S(1)} %get-tuple-element.217), kind=kOutput, calls=%fused_computation.16.clone.1 | convolution fusion | flops 50463360 | bytes 4718769 | tf_op jit(solution)/shard_map/while/body/eval_jaxpr/kf,qfij->kqij/dot_general | solution.py:98
  403.0 6.6 %fusion.86 = f32[1,4,2,128,128]{4,1,3,2,0:T(4,128)S(1)} fusion(f32[2,32,128,128]{3,2,1,0:T(8,128)} %pad_maximum_fusion.6, pred[]{:T(512)S(6)} %ge.54, f32[4]{0:T(128)S(1)} %get-tuple-element.220, s32[32]{0:T(128)S(1)} %get-tuple-element.219, s32[4]{0:T(128)S(1)} %get-tuple-element.218, s32[4]{0:T(128)S(1)} %get-tuple-element.217), kind=kOutput, calls=%fused_computation.16.clone.1 | convolution fusion | flops 50463360 | bytes 4718769 | tf_op jit(solution)/shard_map/while/body/eval_jaxpr/kf,qfij->kqij/dot_general | solution.py:98
  426.9 6.6 %fusion.86 = f32[1,4,2,128,128]{4,1,3,2,0:T(4,128)S(1)} fusion(f32[2,32,128,128]{3,2,1,0:T(8,128)} %pad_maximum_fusion.6, pred[]{:T(512)S(6)} %ge.54, f32[4]{0:T(128)S(1)} %get-tuple-element.220, s32[32]{0:T(128)S(1)} %get-tuple-element.219, s32[4]{0:T(128)S(1)} %get-tuple-element.218, s32[4]{0:T(128)S(1)} %get-tuple-element.217), kind=kOutput, calls=%fused_computation.16.clone.1 | convolution fusion | flops 50463360 | bytes 4718769 | tf_op jit(solution)/shard_map/while/body/eval_jaxpr/kf,qfij->kqij/dot_general | solution.py:98
  450.8 6.6 %fusion.86 = f32[1,4,2,128,128]{4,1,3,2,0:T(4,128)S(1)} fusion(f32[2,32,128,128]{3,2,1,0:T(8,128)} %pad_maximum_fusion.6, pred[]{:T(512)S(6)} %ge.54, f32[4]{0:T(128)S(1)} %get-tuple-element.220, s32[32]{0:T(128)S(1)} %get-tuple-element.219, s32[4]{0:T(128)S(1)} %get-tuple-element.218, s32[4]{0:T(128)S(1)} %get-tuple-element.217), kind=kOutput, calls=%fused_computation.16.clone.1 | convolution fusion | flops 50463360 | bytes 4718769 | tf_op jit(solution)/shard_map/while/body/eval_jaxpr/kf,qfij->kqij/dot_general | solution.py:98
  474.6 6.6 %fusion.86 = f32[1,4,2,128,128]{4,1,3,2,0:T(4,128)S(1)} fusion(f32[2,32,128,128]{3,2,1,0:T(8,128)} %pad_maximum_fusion.6, pred[]{:T(512)S(6)} %ge.54, f32[4]{0:T(128)S(1)} %get-tuple-element.220, s32[32]{0:T(128)S(1)} %get-tuple-element.219, s32[4]{0:T(128)S(1)} %get-tuple-element.218, s32[4]{0:T(128)S(1)} %get-tuple-element.217), kind=kOutput, calls=%fused_computation.16.clone.1 | convolution fusion | flops 50463360 | bytes 4718769 | tf_op jit(solution)/shard_map/while/body/eval_jaxpr/kf,qfij->kqij/dot_general | solution.py:98
  (139 shorter events, 170.8 us)
Async XLA Ops:
  3.3 6.7 %collective-permute-start = (bf16[256,256]{0,1:T(8,128)(2,1)S(1)}, bf16[256,256]{0,1:T(8,128)(2,1)S(1)}, u32[]{:S(2)}, u32[]{:S(2)}) collective-permute-start(bf16[256,256]{0,1:T(8,128)(2,1)S(1)} %slice.80), channel_id=1, source_target_pairs={{32,0},{64,32},{96,64},{128,96},{160,128},{192,160},{224,192},{33,... | collective-permute-start | bytes 393224 | tf_op jit(solution)/shard_map/ppermute | solution.py:23
  33.9 1.4 copy-start.2
  149.6 15.1 %copy-start.3 = (s32[4,2]{0,1:T(2,128)S(1)}, s32[4,2]{0,1:T(2,128)}, u32[]{:S(2)}) copy-start(s32[4,2]{0,1:T(2,128)} %param.7) | copy-start | bytes 100
  156.4 52.1 %collective-permute-start.1 = (bf16[2,2,128,32,128]{4,3,2,1,0:T(8,128)(2,1)}, bf16[2,2,128,32,128]{4,3,2,1,0:T(8,128)(2,1)}, u32[]{:S(2)}, u32[]{:S(2)}) collective-permute-start(bf16[2,2,128,32,128]{4,3,2,1,0:T(8,128)(2,1)} %bitcast.16), channel_id=1, source_target_pairs={{0,1},{1,2},{2,3},{3,4},{4,5},{5,6},{6,7},{7,8},{8,9},{9,10},{10,1... | collective-permute-start | bytes 12582920 | tf_op jit(solution)/shard_map/ppermute | solution.py:34
  162.8 52.2 %collective-permute-start.2 = (bf16[2,2,128,32,128]{4,3,2,1,0:T(8,128)(2,1)}, bf16[2,2,128,32,128]{4,3,2,1,0:T(8,128)(2,1)}, u32[]{:S(2)}, u32[]{:S(2)}) collective-permute-start(bf16[2,2,128,32,128]{4,3,2,1,0:T(8,128)(2,1)} %bitcast.16), channel_id=1, source_target_pairs={{1,0},{2,1},{3,2},{4,3},{5,4},{6,5},{7,6},{8,7},{9,8},{10,9},{11,1... | collective-permute-start | bytes 12582920 | tf_op jit(solution)/shard_map/ppermute | solution.py:36
  225.5 17.9 %copy-start.1 = (s32[10,2]{0,1:T(2,128)S(1)}, s32[10,2]{0,1:T(2,128)}, u32[]{:S(2)}) copy-start(s32[10,2]{0,1:T(2,128)} %param.8) | copy-start | bytes 244
  254.8 1.6 copy-start
  278.7 1.6 copy-start
  302.5 1.6 copy-start
  326.4 1.6 copy-start
  350.3 1.6 copy-start
  374.1 1.6 copy-start
  398.0 1.6 copy-start
  421.8 1.6 copy-start
  445.7 1.6 copy-start
  469.6 1.6 copy-start
where the time goes:
time: 485 us; the launch traced here: 482 us
  local copies, waits for them, and re-layouts  145 us (30%)
  blocking collectives  101 us (21%)
  matrix products  88.8 us (18%)
  other arithmetic  67.9 us (14%)
  waiting for transfers between devices  52.2 us (11%)
  loops' own time  17 us (4%)
  starting transfers between devices  9.56 us (2%)
    all_to_all x1, blocking collectives, shards(): lax.all_to_all(whitened, 'tm', split_axis=3, concat_axis=2, tiled=True)  101 us
    dot_general x10, matrix products, pair_cross(): jnp.einsum('kf,qfij->kqij', weights, stacked, precision=lax.Precision.HIG...  65.6 us
    dynamic_slice x10, local copies, waits for them, and re-layouts, owner_slot(): left_side = lax.dynamic_index_in_dim(window, first_index, 0, keepdims=False)  47.5 us
    ppermute x1, waiting for transfers between devices, extended_2(): lax.ppermute(tail, axis, [(i, (i + 1) % count) for i in range(ends)])  42.7 us
    dynamic_slice x10, local copies, waits for them, and re-layouts, owner_slot(): lax.dynamic_index_in_dim(window, second_index, 0, keepdims=False)  32.2 us
    another operation x10, other arithmetic, pair_cross(): stacked = jnp.stack([real_part, imag_part])  22 us
    unnamed x8, local copies, waits for them, and re-layouts  21.2 us
    slice x10, other arithmetic, pair_cross(): swapped = jnp.stack([left_side[1], -left_side[0]])  17.5 us
  transfers between devices with their start and end apart: 3, of which 3 were waited for; matrix products, arithmetic and copies ran while one was open for 1% of the time, Pallas kernels for 0%

commit v1 on v0

v1 whole, which is shorter than its diff:
```python
import functools

import jax
import jax.numpy as jnp
import numpy as np
from jax import lax
from jax.experimental import pallas as pl
from jax.experimental.pallas import tpu as pltpu
from jax.sharding import PartitionSpec as P

CB = 128
SEG = 512
HALF = 256
NF = 256
SMOOTH = 64
LANES = 128
RUNS = 8
BINS = 32
GROUPS = 4
JG = 4
BANDS_DEV = 4
ROWS = 10
HOPS = (0, 4, 3, 5, 2, 6, 1, 7)

whiten_eps = 1e-06
MESH = pl.DeviceIdType.MESH


def constant_tables():
    n = np.arange(SEG)[:, None].astype(np.int64)
    f = np.arange(NF)[None, :].astype(np.int64)
    phase = (n * f % SEG).astype(np.float64) * (2.0 * np.pi / SEG)
    taper = 0.5 - 0.5 * np.cos(np.arange(SEG).astype(np.float64) * (2.0 * np.pi / SEG))
    tables = np.concatenate([taper[:, None] * np.cos(phase), -taper[:, None] * np.sin(phase)], axis=1)
    bins = np.arange(NF)
    near = (np.abs(bins[:, None] - bins[None, :]) <= SMOOTH).astype(np.float32)
    counts = near.sum(axis=0)
    inverse = np.broadcast_to((1.0 / counts).astype(np.float32)[None, :], (8, NF))
    return (
        jnp.asarray(tables.astype(np.float32), jnp.bfloat16),
        jnp.asarray(near, jnp.bfloat16),
        jnp.asarray(inverse, jnp.float32),
    )


def kernel(
    edges, slots, traces, tables, near, inverse, out,
    xh, tab, ban, inv, spec, send, big, acc, masks, stage,
    load_sem, halo_sem, out_sem, send_sem, recv_sem, fsend_sem, frecv_sem,
):
    t = lax.axis_index("tm")
    ch = lax.axis_index("chan")
    chans = 32
    samples = 4096

    loads = [
        pltpu.make_async_copy(tables, tab, load_sem.at[0]),
        pltpu.make_async_copy(near, ban, load_sem.at[1]),
        pltpu.make_async_copy(inverse, inv, load_sem.at[2]),
        pltpu.make_async_copy(traces, xh.at[:, pl.ds(0, samples)], load_sem.at[3]),
    ]
    for load in loads:
        load.start()

    def tm_at(step):
        return lax.rem(t + step, RUNS)

    right = lax.rem(ch + 1, chans)
    left = lax.rem(ch + chans - 1, chans)

    barrier = pltpu.get_barrier_semaphore()
    for hop in range(1, RUNS):
        pl.semaphore_signal(barrier, inc=1, device_id=(tm_at(hop), ch), device_id_type=MESH)
    pl.semaphore_signal(barrier, inc=1, device_id=(t, right), device_id_type=MESH)
    pl.semaphore_signal(barrier, inc=1, device_id=(t, left), device_id_type=MESH)
    pl.semaphore_wait(barrier, RUNS + 1)

    halo = pltpu.make_async_remote_copy(
        src_ref=traces.at[:, pl.ds(0, HALF)],
        dst_ref=xh.at[:, pl.ds(samples, HALF)],
        send_sem=halo_sem.at[0],
        recv_sem=halo_sem.at[1],
        device_id=(tm_at(RUNS - 1), ch),
        device_id_type=MESH,
    )
    halo.start()
    for load in loads:
        load.wait()

    def run_copy(place, g, b):
        run = tm_at(HOPS[place])
        return pltpu.make_async_remote_copy(
            src_ref=send.at[run, g, b],
            dst_ref=big.at[place, g, 2 + b],
            send_sem=send_sem.at[place, g, b],
            recv_sem=recv_sem.at[place, g, b],
            device_id=(run, ch),
            device_id_type=MESH,
        )

    def own_copy(g, b):
        return pltpu.make_async_copy(send.at[t, g, b], big.at[0, g, 2 + b], recv_sem.at[0, g, b])

    def forward(side, place, g):
        return pltpu.make_async_remote_copy(
            src_ref=big.at[place, g, pl.ds(2, 2)],
            dst_ref=big.at[place, g, pl.ds(4 * side, 2)],
            send_sem=fsend_sem.at[side, place, g],
            recv_sem=frecv_sem.at[side, place, g],
            device_id=(t, left if side else right),
            device_id_type=MESH,
        )

    lane_group = lax.broadcasted_iota(jnp.int32, (CB, LANES), 1) // BINS
    low_half = lane_group < 2
    even_part = lane_group % 2 == 0

    def transform(step, carry):
        g = step // 2
        b = step % 2

        @pl.when(step == 2 * (GROUPS - 1))
        def _():
            halo.wait()

            @pl.when(t == RUNS - 1)
            def _():
                xh[:, pl.ds(samples, HALF)] = jnp.zeros((2 * CB, HALF), jnp.bfloat16)

        rows = pl.ds(pl.multiple_of(b * CB, CB), CB)
        frames = jnp.concatenate(
            [
                xh[rows, pl.ds(pl.multiple_of(g * (JG * HALF) + jj * HALF, HALF), SEG)]
                for jj in range(JG)
            ],
            axis=0,
        )
        spec[...] = jnp.dot(frames, tab[...], preferred_element_type=jnp.float32)
        for jj in range(JG):
            part = pl.ds(jj * CB, CB)
            real = spec[part, pl.ds(0, NF)]
            imag = spec[part, pl.ds(NF, NF)]
            power = real * real + imag * imag
            head = power.astype(jnp.bfloat16)
            rest = (power - head.astype(jnp.float32)).astype(jnp.bfloat16)
            total = jnp.dot(head, ban[...], preferred_element_type=jnp.float32)
            total += jnp.dot(rest, ban[...], preferred_element_type=jnp.float32)
            scale = lax.rsqrt(total * inv[0:1, :] + whiten_eps)
            spec[part, pl.ds(0, NF)] = real * scale
            spec[part, pl.ds(NF, NF)] = imag * scale
        for q in range(2):
            for h in range(2):
                column = pl.ds(q * NF + h * LANES, LANES)
                tiles = [spec[pl.ds(jj * CB, CB), column] for jj in range(JG)]

                def swap(a, c, mask, by):
                    return (
                        jnp.where(mask, a, pltpu.roll(c, by, 1)),
                        jnp.where(mask, pltpu.roll(a, LANES - by, 1), c),
                    )

                t0, t2 = swap(tiles[0], tiles[2], low_half, 2 * BINS)
                t1, t3 = swap(tiles[1], tiles[3], low_half, 2 * BINS)
                u0, u1 = swap(t0, t1, even_part, BINS)
                u2, u3 = swap(t2, t3, even_part, BINS)
                for s, tile in enumerate((u0, u1, u2, u3)):
                    send[h * 4 + s, g, b, q] = tile.astype(jnp.bfloat16)
        own_copy(g, b).start()
        for place in range(1, RUNS):
            run_copy(place, g, b).start()
        return carry

    lax.fori_loop(0, 2 * GROUPS, transform, 0)

    base = edges[0, 0]
    bin_ids = lax.broadcasted_iota(jnp.int32, (CB, LANES), 1) % BINS
    for k in range(BANDS_DEV):
        inside = (bin_ids >= edges[k, 0] - base) & (bin_ids < edges[k, 1] - base)
        masks[k] = inside.astype(jnp.float32).astype(jnp.bfloat16)
    acc[...] = jnp.zeros_like(acc)

    def receive(step):
        g = step // 2
        for half in range(2):
            @pl.when(step % 2 == half)
            def _():
                for place in range(4 * half, 4 * half + 4):
                    for b in range(2):
                        if place == 0:
                            own_copy(g, b).wait()
                        else:
                            run_copy(place, g, b).wait_recv()
                    forward(0, place, g).start()
                    forward(1, place, g).start()

    def multiply(step):
        g = step // 2
        first = (step % 2) * 4
        for side in range(2):
            for i in range(4):
                forward(side, first + i, g).wait_recv()

        def one_left(i, carry):
            side = i // 4
            block = i - 2 * side
            base_right = 2 + 2 * side
            rights = jnp.concatenate(
                [
                    jnp.concatenate(
                        [big[first + p, g, base_right + n, q] for p in range(4) for q in range(2)],
                        axis=1,
                    )
                    for n in range(2)
                ],
                axis=0,
            )
            for k in range(BANDS_DEV):
                mask = masks[k]
                pieces_re = []
                pieces_im = []
                for p in range(4):
                    l0 = big[first + p, g, block, 0] * mask
                    l1 = big[first + p, g, block, 1] * mask
                    pieces_re += [l0, l1]
                    pieces_im += [l1, -l0]
                both = jnp.concatenate(
                    [jnp.concatenate(pieces_re, axis=1), jnp.concatenate(pieces_im, axis=1)], axis=0
                )
                sums = lax.dot_general(
                    both, rights, (((1,), (1,)), ((), ())), preferred_element_type=jnp.float32
                )
                for n in range(2):
                    for q in range(2):
                        acc[2 * i + n, k, q] += sums[q * CB:(q + 1) * CB, n * CB:(n + 1) * CB]
            return carry

        lax.fori_loop(0, 6, one_left, 0)

    receive(0)

    def steps(step, carry):
        receive(step)
        multiply(step - 1)
        return carry

    lax.fori_loop(1, 2 * GROUPS, steps, 0)
    multiply(2 * GROUPS - 1)

    first_block = 2 * ch - 2
    scales = []
    for k in range(BANDS_DEV):
        width = jnp.full((8, LANES), edges[k, 1] - edges[k, 0], jnp.int32).astype(jnp.float32)
        scales.append((1.0 / jnp.sqrt(128.0 * width))[0:1, :])
    for r in range(ROWS):
        a = slots[r, 0]
        l = jnp.clip(a - first_block, 0, 3)
        n = jnp.clip(slots[r, 1] - first_block, 2, 5)
        far = n >= 4
        index = jnp.clip(jnp.where(far, 2 * (l + 2) + n - 4, 2 * l + n - 2), 0, 11)
        live = a >= 0
        for k in range(BANDS_DEV):
            for q in range(2):
                value = acc[index, k, q] * scales[k]
                stage[r, k, q] = jnp.where(live, value, 0.0)
        pltpu.make_async_copy(stage.at[r], out.at[r], out_sem.at[r]).start()

    def drain(step, carry):
        g = step // 2
        b = step % 2
        for place in range(1, RUNS):
            run_copy(place, g, b).wait_send()
        return carry

    lax.fori_loop(0, 2 * GROUPS, drain, 0)

    def drain_forward(g, carry):
        for place in range(RUNS):
            forward(0, place, g).wait_send()
            forward(1, place, g).wait_send()
        return carry

    lax.fori_loop(0, GROUPS, drain_forward, 0)
    for r in range(ROWS):
        pltpu.make_async_copy(stage.at[r], out.at[r], out_sem.at[r]).wait()


def shards(traces, band_edges, slot_pairs):
    tables, near, inverse = constant_tables()
    smem = pl.BlockSpec(memory_space=pltpu.SMEM)
    hbm = pl.BlockSpec(memory_space=pl.ANY)
    bf16 = jnp.bfloat16
    return pl.pallas_call(
        kernel,
        out_shape=jax.ShapeDtypeStruct((ROWS, BANDS_DEV, 2, CB, CB), jnp.float32),
        in_specs=[smem, smem, hbm, hbm, hbm, hbm],
        out_specs=hbm,
        scratch_shapes=[
            pltpu.VMEM((2 * CB, 4096 + HALF), bf16),
            pltpu.VMEM((SEG, 2 * NF), bf16),
            pltpu.VMEM((NF, NF), bf16),
            pltpu.VMEM((8, NF), jnp.float32),
            pltpu.VMEM((JG * CB, 2 * NF), jnp.float32),
            pltpu.VMEM((RUNS, GROUPS, 2, 2, CB, LANES), bf16),
            pltpu.VMEM((RUNS, GROUPS, 6, 2, CB, LANES), bf16),
            pltpu.VMEM((12, BANDS_DEV, 2, CB, CB), jnp.float32),
            pltpu.VMEM((BANDS_DEV, CB, LANES), bf16),
            pltpu.VMEM((ROWS, BANDS_DEV, 2, CB, CB), jnp.float32),
            pltpu.SemaphoreType.DMA((4,)),
            pltpu.SemaphoreType.DMA((2,)),
            pltpu.SemaphoreType.DMA((ROWS,)),
            pltpu.SemaphoreType.DMA((RUNS, GROUPS, 2)),
            pltpu.SemaphoreType.DMA((RUNS, GROUPS, 2)),
            pltpu.SemaphoreType.DMA((2, RUNS, GROUPS)),
            pltpu.SemaphoreType.DMA((2, RUNS, GROUPS)),
        ],
        compiler_params=pltpu.CompilerParams(
            collective_id=0, has_side_effects=True, vmem_limit_bytes=56 * 2**20
        ),
        name="cross_spectra",
    )(band_edges, slot_pairs, traces, tables, near, inverse)


def solution(mesh):
    in_specs = (P("chan", "tm"), P("tm", None), P("chan", None))
    out_specs = P("chan", "tm", None, None, None)
    return jax.shard_map(shards, mesh=mesh, in_specs=in_specs, out_specs=out_specs, check_vma=False)
```

time: 485 us -> 134 us (0.28)
  local copies, waits for them, and re-layouts: 145 us -> 9.45 us
  Pallas kernels: 0 us -> 122 us
  blocking collectives: 101 us -> 0 us
  matrix products: 88.8 us -> 0 us
  other arithmetic: 67.9 us -> 0 us
  waiting for transfers between devices: 52.2 us -> 0 us
  loops' own time: 17 us -> 0 us
  starting transfers between devices: 9.56 us -> 0 us
    pallas_call x0 -> x1, Pallas kernels: none -> 122 us  [shards(): pl.pallas_call(kernel, out_shape=jax.ShapeDtypeStruct((ROWS, BANDS_DEV, 2...]
    all_to_all x1 -> x0, blocking collectives: 101 us -> none  [shards(): lax.all_to_all(whitened, 'tm', split_axis=3, concat_axis=2, tiled=True)]
    dot_general x31 -> x0, matrix products: 88.8 us -> none  [the longest x10 65.6 us: pair_cross(): jnp.einsum('kf,qfij->kqij', weights, stacked, precision=lax.Precision.HIG...]
    dynamic_slice x30 -> x0, local copies, waits for them, and re-layouts: 80.4 us -> none  [the longest x10 47.5 us: owner_slot(): left_side = lax.dynamic_index_in_dim(window, first_index, 0, keepdims=False)]
    ppermute x3 -> x0, waiting for transfers between devices: 52.2 us -> none  [the longest x1 42.7 us: extended_2(): lax.ppermute(tail, axis, [(i, (i + 1) % count) for i in range(ends)])]
    another operation x14 -> x0, other arithmetic: 27.3 us -> none  [the longest x10 22 us: pair_cross(): stacked = jnp.stack([real_part, imag_part])]
    slice x10 -> x0, other arithmetic: 17.5 us -> none  [pair_cross(): swapped = jnp.stack([left_side[1], -left_side[0]])]
    another operation x1 -> x0, loops' own time: 17 us -> none  [shards(): cross_spectra = lax.map(owner_slot, slot_pairs)]
  transfers between devices with their start and end apart: 3 -> 0, of which waited for: 3 -> 0; matrix products, arithmetic and copies ran while one was open for 1% -> 0% of each run, Pallas kernels for 0% -> 0%
where the time goes in v1:
time: 134 us; the launch traced here: 132 us
  Pallas kernels  122 us (91%)
  local copies, waits for them, and re-layouts  9.45 us (7%)
    pallas_call x1, Pallas kernels, shards(): pl.pallas_call(kernel, out_shape=jax.ShapeDtypeStruct((ROWS, BANDS_DEV, 2...  122 us
    unnamed x3, local copies, waits for them, and re-layouts  8.18 us

profile of v1, /device:TPU:25, one launch (start us, length us, event | category | flops | bytes accessed | tf_op | source)
XLA Modules:
  0.0 131.9 jit_solution(13085409953057064299)
XLA Ops:
  0.0 1.3 %copy.7.edges = s32[4,2]{1,0:T(4,128)} copy(s32[4,2]{0,1:T(2,128)} %param.7) | data formatting | bytes 64 | tf_op args[1]
  1.3 1.4 %copy.8.slots = s32[10,2]{1,0:T(8,128)} copy(s32[10,2]{0,1:T(2,128)} %param.8) | data formatting | bytes 160 | tf_op args[2]
  2.7 1.3 jit_solution_.3.inverse
  4.0 122.5 %cross_spectra.1 = f32[10,4,2,128,128]{4,3,2,1,0:T(8,128)} custom-call(s32[4,2]{1,0:T(4,128)} %copy.7.edges, s32[10,2]{1,0:T(8,128)} %copy.8.slots, bf16[256,4096]{1,0:T(8,128)(2,1)} %traces.1, bf16[512,512]{1,0:T(8,128)(2,1)} %constant.6.clone.tables, bf16[256,256]{1,0:T(8,128)(2,1)} %constant.7.clone.near, f32[8,256]{1,0:T(8,128)} %jit_solution_.3.inverse), custom_call_target="tpu_custom_call" | custom-call | tf_op jit(solution)/shard_map/cross_spectra/pallas_call | solution.py:292
  126.5 5.5 %copy.10 = f32[10,4,2,128,128]{4,3,2,1,0:T(8,128)} copy(f32[10,4,2,128,128]{4,3,2,1,0:T(8,128)} %cross_spectra.1) | data formatting | bytes 10485760

commit v2 on v1

v2 whole, which is shorter than its diff:
```python
import functools

import jax
import jax.numpy as jnp
import numpy as np
from jax import lax
from jax.experimental import pallas as pl
from jax.experimental.pallas import tpu as pltpu
from jax.sharding import PartitionSpec as P

CB = 128
SEG = 512
HALF = 256
NF = 256
SMOOTH = 64
LANES = 128
RUNS = 8
BINS = 32
GROUPS = 4
JG = 4
BANDS_DEV = 4
ROWS = 10
HOPS = (0, 4, 3, 5, 2, 6, 1, 7)
PAIRS = 4
UNITS = GROUPS * PAIRS
AHEAD = 3
LATER = 3

whiten_eps = 1e-06
MESH = pl.DeviceIdType.MESH


def constant_tables():
    n = np.arange(SEG)[:, None].astype(np.int64)
    f = np.arange(NF)[None, :].astype(np.int64)
    phase = (n * f % SEG).astype(np.float64) * (2.0 * np.pi / SEG)
    taper = 0.5 - 0.5 * np.cos(np.arange(SEG).astype(np.float64) * (2.0 * np.pi / SEG))
    tables = np.concatenate([taper[:, None] * np.cos(phase), -taper[:, None] * np.sin(phase)], axis=1)
    bins = np.arange(NF)
    near = (np.abs(bins[:, None] - bins[None, :]) <= SMOOTH).astype(np.float32)
    return (
        jnp.asarray(tables.astype(np.float32), jnp.bfloat16),
        jnp.asarray(near, jnp.bfloat16),
    )


def cross_kernel(
    edges_hbm, traces, tables, near, acc,
    edges, xh, tab, ban, spec, send, big, masks,
    load_sem, halo_sem, send_sem, recv_sem, fsend_sem, frecv_sem,
):
    t = lax.axis_index("tm")
    ch = lax.axis_index("chan")
    chans = 32
    samples = 4096
    early = (JG + 1) * HALF

    loads = [
        pltpu.make_async_copy(tables, tab, load_sem.at[0]),
        pltpu.make_async_copy(
            traces.at[:, pl.ds(0, early)], xh.at[:, pl.ds(0, early)], load_sem.at[1]
        ),
        pltpu.make_async_copy(near, ban, load_sem.at[2]),
        pltpu.make_async_copy(
            traces.at[:, pl.ds(early, samples - early)],
            xh.at[:, pl.ds(early, samples - early)],
            load_sem.at[3],
        ),
        pltpu.make_async_copy(edges_hbm, edges, load_sem.at[4]),
    ]
    for load in loads:
        load.start()

    def tm_at(step):
        return lax.rem(t + step, RUNS)

    right = lax.rem(ch + 1, chans)
    left = lax.rem(ch + chans - 1, chans)

    barrier = pltpu.get_barrier_semaphore()
    for hop in range(1, RUNS):
        pl.semaphore_signal(barrier, inc=1, device_id=(tm_at(hop), ch), device_id_type=MESH)
    pl.semaphore_signal(barrier, inc=1, device_id=(t, right), device_id_type=MESH)
    pl.semaphore_signal(barrier, inc=1, device_id=(t, left), device_id_type=MESH)

    halo = pltpu.make_async_remote_copy(
        src_ref=traces.at[:, pl.ds(0, HALF)],
        dst_ref=xh.at[:, pl.ds(samples, HALF)],
        send_sem=halo_sem.at[0],
        recv_sem=halo_sem.at[1],
        device_id=(tm_at(RUNS - 1), ch),
        device_id_type=MESH,
    )

    def run_copy(place, g, b):
        run = tm_at(HOPS[place])
        return pltpu.make_async_remote_copy(
            src_ref=send.at[run, g, b],
            dst_ref=big.at[place, g, 2 + b],
            send_sem=send_sem.at[place, g, b],
            recv_sem=recv_sem.at[place, g, b],
            device_id=(run, ch),
            device_id_type=MESH,
        )

    def own_copy(g, b):
        return pltpu.make_async_copy(send.at[t, g, b], big.at[0, g, 2 + b], recv_sem.at[0, g, b])

    def forward(side, place, g, b):
        return pltpu.make_async_remote_copy(
            src_ref=big.at[place, g, 2 + b],
            dst_ref=big.at[place, g, 4 * side + b],
            send_sem=fsend_sem.at[side, place, g, b],
            recv_sem=frecv_sem.at[side, place, g, b],
            device_id=(t, left if side else right),
            device_id_type=MESH,
        )

    lane = lax.broadcasted_iota(jnp.int32, (CB, LANES), 1)
    lane_group = lane // BINS
    low_half = lane_group < 2
    even_part = lane_group % 2 == 0
    bin_row = lax.broadcasted_iota(jnp.int32, (1, NF), 1)
    count = jnp.minimum(bin_row + SMOOTH + 1, NF) - jnp.maximum(bin_row - SMOOTH, 0)
    inverse = 1.0 / count.astype(jnp.float32)

    def transform(g, b):
        rows = pl.ds(pl.multiple_of(b * CB, CB), CB)
        frames = jnp.concatenate(
            [
                xh[rows, pl.ds(pl.multiple_of(g * (JG * HALF) + jj * HALF, HALF), SEG)]
                for jj in range(JG)
            ],
            axis=0,
        )
        spec[...] = jnp.dot(frames, tab[...], preferred_element_type=jnp.float32)
        for jj in range(JG):
            part = pl.ds(jj * CB, CB)
            real = spec[part, pl.ds(0, NF)]
            imag = spec[part, pl.ds(NF, NF)]
            power = real * real + imag * imag
            head = power.astype(jnp.bfloat16)
            rest = (power - head.astype(jnp.float32)).astype(jnp.bfloat16)
            total = jnp.dot(head, ban[...], preferred_element_type=jnp.float32)
            total += jnp.dot(rest, ban[...], preferred_element_type=jnp.float32)
            scale = lax.rsqrt(total * inverse + whiten_eps)
            spec[part, pl.ds(0, NF)] = real * scale
            spec[part, pl.ds(NF, NF)] = imag * scale
        for q in range(2):
            for h in range(2):
                column = pl.ds(q * NF + h * LANES, LANES)
                tiles = [spec[pl.ds(jj * CB, CB), column] for jj in range(JG)]

                def swap(a, c, mask, by):
                    return (
                        jnp.where(mask, a, pltpu.roll(c, by, 1)),
                        jnp.where(mask, pltpu.roll(a, LANES - by, 1), c),
                    )

                t0, t2 = swap(tiles[0], tiles[2], low_half, 2 * BINS)
                t1, t3 = swap(tiles[1], tiles[3], low_half, 2 * BINS)
                u0, u1 = swap(t0, t1, even_part, BINS)
                u2, u3 = swap(t2, t3, even_part, BINS)
                for s, tile in enumerate((u0, u1, u2, u3)):
                    send[h * 4 + s, g, b, q] = tile.astype(jnp.bfloat16)

    def both_blocks(g):
        def block(b, carry):
            transform(g, b)
            return carry

        lax.fori_loop(0, 2, block, 0)

    def places(pair):
        return (2 * pair, 2 * pair + 1)

    def send_unit(unit):
        g = unit // PAIRS
        for pair in range(PAIRS):
            @pl.when(unit % PAIRS == pair)
            def _():
                for b in range(2):
                    for place in places(pair):
                        if place:
                            run_copy(place, g, b).start()

    for load in loads[:3]:
        load.wait()
    both_blocks(0)
    pl.semaphore_wait(barrier, RUNS + 1)
    halo.start()
    for unit in range(AHEAD):
        send_unit(jnp.int32(unit))
    for b in range(2):
        own_copy(0, b).start()
    loads[3].wait()
    loads[4].wait()

    def later_group(g, carry):
        @pl.when(g == GROUPS - 1)
        def _():
            halo.wait()

            @pl.when(t == RUNS - 1)
            def _():
                xh[:, pl.ds(samples, HALF)] = jnp.zeros((2 * CB, HALF), jnp.bfloat16)

        both_blocks(g)
        for b in range(2):
            own_copy(g, b).start()
        return carry

    lax.fori_loop(1, GROUPS, later_group, 0)

    base = edges[0, 0]
    bin_ids = lane % BINS
    for k in range(BANDS_DEV):
        inside = (bin_ids >= edges[0, k] - base) & (bin_ids < edges[1, k] - base)
        masks[k] = inside.astype(jnp.float32).astype(jnp.bfloat16)
    acc[...] = jnp.zeros_like(acc)

    def receive(unit):
        g = unit // PAIRS
        for pair in range(PAIRS):
            @pl.when(unit % PAIRS == pair)
            def _():
                for b in range(2):
                    for place in places(pair):
                        if place == 0:
                            own_copy(g, b).wait()
                        else:
                            run_copy(place, g, b).wait_recv()
                        forward(0, place, g, b).start()
                        forward(1, place, g, b).start()

        @pl.when(unit + AHEAD < UNITS)
        def _():
            send_unit(unit + AHEAD)

    def wait_neighbours(unit):
        g = unit // PAIRS
        first = 2 * (unit % PAIRS)
        for b in range(2):
            for i in range(2):
                for side in range(2):
                    forward(side, first + i, g, b).wait_recv()

    def multiply(unit, count, place_of):
        g = unit // PAIRS
        first = 2 * (unit % PAIRS)

        def one_left(item, carry):
            i = place_of(item)
            side = i // 4
            block = i - 2 * side
            base_right = 2 + 2 * side
            rights = jnp.concatenate(
                [
                    jnp.concatenate(
                        [big[first + p, g, base_right + n, q] for p in range(2) for q in range(2)],
                        axis=1,
                    )
                    for n in range(2)
                ],
                axis=0,
            )
            for k in range(BANDS_DEV):
                mask = masks[k]
                pieces_re = []
                pieces_im = []
                for p in range(2):
                    l0 = big[first + p, g, block, 0] * mask
                    l1 = big[first + p, g, block, 1] * mask
                    pieces_re += [l0, l1]
                    pieces_im += [l1, -l0]
                both = jnp.concatenate(
                    [jnp.concatenate(pieces_re, axis=1), jnp.concatenate(pieces_im, axis=1)], axis=0
                )
                sums = lax.dot_general(
                    both, rights, (((1,), (1,)), ((), ())), preferred_element_type=jnp.float32
                )
                for n in range(2):
                    for q in range(2):
                        acc[2 * i + n, k, q] += sums[q * CB:(q + 1) * CB, n * CB:(n + 1) * CB]
            return carry

        lax.fori_loop(0, count, one_left, 0)

    def multiply_own(unit):
        multiply(unit, 2, lambda item: item + 2)

    def multiply_neighbours(unit):
        wait_neighbours(unit)
        multiply(unit, 4, lambda item: item + 2 * (item // 2))

    def drain(unit):
        g = unit // PAIRS
        for pair in range(PAIRS):
            @pl.when(unit % PAIRS == pair)
            def _():
                for place in places(pair):
                    for b in range(2):
                        if place:
                            run_copy(place, g, b).wait_send()
                        forward(0, place, g, b).wait_send()
                        forward(1, place, g, b).wait_send()

    def steps(unit, carry):
        receive(unit)
        multiply_own(unit)

        @pl.when(unit >= 1)
        def _():
            multiply_neighbours(unit - 1)

        @pl.when(unit >= LATER)
        def _():
            drain(unit - LATER)

        return carry

    lax.fori_loop(0, UNITS, steps, 0)
    multiply_neighbours(UNITS - 1)

    def drain_last(unit, carry):
        drain(unit)
        return carry

    lax.fori_loop(UNITS - LATER, UNITS, drain_last, 0)


def rows_kernel(edges, slots, acc, out, stage, out_sem):
    first_block = 2 * lax.axis_index("chan") - 2
    scales = []
    for k in range(BANDS_DEV):
        width = jnp.full((1, LANES), edges[1, k] - edges[0, k], jnp.int32).astype(jnp.float32)
        scales.append(1.0 / jnp.sqrt(128.0 * width))

    def row_copy(r):
        return pltpu.make_async_copy(stage.at[r], out.at[r], out_sem.at[r])

    def one_row(r, carry):
        a = slots[0, r]
        l = jnp.clip(a - first_block, 0, 3)
        n = jnp.clip(slots[1, r] - first_block, 2, 5)
        index = jnp.clip(jnp.where(n >= 4, 2 * (l + 2) + n - 4, 2 * l + n - 2), 0, 11)
        live = a >= 0
        for k in range(BANDS_DEV):
            for q in range(2):
                stage[r, k, q] = jnp.where(live, acc[index, k, q] * scales[k], 0.0)
        row_copy(r).start()
        return carry

    lax.fori_loop(0, ROWS, one_row, 0)
    for r in range(ROWS):
        row_copy(r).wait()


def shards(traces, band_edges, slot_pairs):
    tables, near = constant_tables()
    edges, slots = band_edges.T, slot_pairs.T
    smem = pl.BlockSpec(memory_space=pltpu.SMEM)
    vmem = pl.BlockSpec(memory_space=pltpu.VMEM)
    hbm = pl.BlockSpec(memory_space=pltpu.HBM)
    anywhere = pl.BlockSpec(memory_space=pl.ANY)
    bf16 = jnp.bfloat16
    traces = pltpu.with_memory_space_constraint(traces, pltpu.HBM)
    sums_shape = (12, BANDS_DEV, 2, CB, CB)
    sums = pl.pallas_call(
        cross_kernel,
        out_shape=pltpu.VMEM(sums_shape, jnp.float32),
        in_specs=[hbm, hbm, anywhere, anywhere],
        out_specs=vmem,
        scratch_shapes=[
            pltpu.SMEM((2, BANDS_DEV), jnp.int32),
            pltpu.VMEM((2 * CB, 4096 + HALF), bf16),
            pltpu.VMEM((SEG, 2 * NF), bf16),
            pltpu.VMEM((NF, NF), bf16),
            pltpu.VMEM((JG * CB, 2 * NF), jnp.float32),
            pltpu.VMEM((RUNS, GROUPS, 2, 2, CB, LANES), bf16),
            pltpu.VMEM((RUNS, GROUPS, 6, 2, CB, LANES), bf16),
            pltpu.VMEM((BANDS_DEV, CB, LANES), bf16),
            pltpu.SemaphoreType.DMA((5,)),
            pltpu.SemaphoreType.DMA((2,)),
            pltpu.SemaphoreType.DMA((RUNS, GROUPS, 2)),
            pltpu.SemaphoreType.DMA((RUNS, GROUPS, 2)),
            pltpu.SemaphoreType.DMA((2, RUNS, GROUPS, 2)),
            pltpu.SemaphoreType.DMA((2, RUNS, GROUPS, 2)),
        ],
        compiler_params=pltpu.CompilerParams(
            collective_id=0, has_side_effects=True, vmem_limit_bytes=56 * 2**20
        ),
        name="cross_spectra",
    )(pltpu.with_memory_space_constraint(edges, pltpu.HBM), traces, tables, near)
    sums = pltpu.with_memory_space_constraint(sums, pltpu.VMEM)
    return pl.pallas_call(
        rows_kernel,
        out_shape=jax.ShapeDtypeStruct((ROWS, BANDS_DEV, 2, CB, CB), jnp.float32),
        in_specs=[smem, smem, vmem],
        out_specs=anywhere,
        scratch_shapes=[
            pltpu.VMEM((ROWS, BANDS_DEV, 2, CB, CB), jnp.float32),
            pltpu.SemaphoreType.DMA((ROWS,)),
        ],
        compiler_params=pltpu.CompilerParams(vmem_limit_bytes=16 * 2**20),
        name="output_rows",
    )(edges, slots, sums)


def solution(mesh):
    in_specs = (P("chan", "tm"), P("tm", None), P("chan", None))
    out_specs = P("chan", "tm", None, None, None)
    return jax.shard_map(shards, mesh=mesh, in_specs=in_specs, out_specs=out_specs, check_vma=False)
```

time: 134 us -> 119 us (0.89)
  local copies, waits for them, and re-layouts: 9.45 us -> 0.01 us
  Pallas kernels: 122 us -> 118 us
    unnamed x3 -> x4, local copies, waits for them, and re-layouts: 8.18 us -> 0.01 us
    pallas_call x1 -> x2, Pallas kernels: 122 us -> 118 us  [the longest x1 115 us: shards(): pl.pallas_call(cross_kernel, out_shape=pltpu.VMEM(sums_shape, jnp.float32...]
where the time goes in v2:
time: 119 us; the launch traced here: 118 us
  Pallas kernels  118 us (99%)
    pallas_call x1, Pallas kernels, shards(): pl.pallas_call(cross_kernel, out_shape=pltpu.VMEM(sums_shape, jnp.float32...  115 us
    pallas_call x1, Pallas kernels, shards(): pl.pallas_call(rows_kernel, out_shape=jax.ShapeDtypeStruct((ROWS, BANDS_D...  3.04 us

profile of v2, /device:TPU:25, one launch (start us, length us, event | category | flops | bytes accessed | tf_op | source)
XLA Modules:
  0.0 117.6 jit_solution(10064543892498224277)
XLA Ops:
  0.0 0.0 copy-start.1
  0.0 0.0 copy-start
  0.0 114.5 %cross_spectra.1.acc = f32[12,4,2,128,128]{4,3,2,1,0:T(8,128)S(1)} custom-call(s32[2,4]{1,0:T(2,128)} %bitcast.2, bf16[256,4096]{1,0:T(8,128)(2,1)} %traces.1, bf16[512,512]{1,0:T(8,128)(2,1)} %constant.4.clone.tables, bf16[256,256]{1,0:T(8,128)(2,1)} %constant.5.clone.near), custom_call_target="tpu_custom_call" | custom-call | tf_op jit(solution)/shard_map/cross_spectra/pallas_call | solution.py:369
  114.6 0.0 copy-done.1
  114.6 0.0 copy-done
  114.6 3.0 %output_rows.1 = f32[10,4,2,128,128]{4,3,2,1,0:T(8,128)} custom-call(s32[2,4]{1,0:T(2,128)S(1)} %bitcast.3, s32[2,10]{1,0:T(2,128)S(1)} %bitcast.4, f32[12,4,2,128,128]{4,3,2,1,0:T(8,128)S(1)} %cross_spectra.1.acc), custom_call_target="tpu_custom_call" | custom-call | tf_op jit(solution)/shard_map/output_rows/pallas_call | solution.py:396
Async XLA Ops:
  0.0 114.6 %copy-start.1 = (s32[10,2]{0,1:T(2,128)S(1)}, s32[10,2]{0,1:T(2,128)}, u32[]{:S(2)}) copy-start(s32[10,2]{0,1:T(2,128)} %param.7) | copy-start | bytes 244
  0.0 114.6 %copy-start = (s32[4,2]{0,1:T(2,128)S(1)}, s32[4,2]{0,1:T(2,128)}, u32[]{:S(2)}) copy-start(s32[4,2]{0,1:T(2,128)} %param.6) | copy-start | bytes 100

commit v3 on v2

--- a/solution.py
+++ b/solution.py
@@ -20,11 +20,10 @@
 JG = 4
 BANDS_DEV = 4
 ROWS = 10
-HOPS = (0, 4, 3, 5, 2, 6, 1, 7)
-PAIRS = 4
-UNITS = GROUPS * PAIRS
-AHEAD = 3
-LATER = 3
+SLOTS = RUNS * GROUPS
+PAIRED = SLOTS - GROUPS
+AHEAD = 16
+LATER = 6
 
 whiten_eps = 1e-06
 MESH = pl.DeviceIdType.MESH
@@ -92,26 +91,33 @@
         device_id_type=MESH,
     )
 
-    def run_copy(place, g, b):
-        run = tm_at(HOPS[place])
+    def route(slot):
+        near = (slot - GROUPS) // RUNS + 1
+        place = (slot - GROUPS) % RUNS
+        far = slot // PAIRED
+        hop = near + (slot % 2) * (RUNS - 2 * near)
+        return tm_at(hop), far * place + (1 - far) * (place // 2)
+
+    def run_copy(slot, b):
+        run, g = route(slot)
         return pltpu.make_async_remote_copy(
             src_ref=send.at[run, g, b],
-            dst_ref=big.at[place, g, 2 + b],
-            send_sem=send_sem.at[place, g, b],
-            recv_sem=recv_sem.at[place, g, b],
+            dst_ref=big.at[slot, 2 + b],
+            send_sem=send_sem.at[slot, b],
+            recv_sem=recv_sem.at[slot, b],
             device_id=(run, ch),
             device_id_type=MESH,
         )
 
     def own_copy(g, b):
-        return pltpu.make_async_copy(send.at[t, g, b], big.at[0, g, 2 + b], recv_sem.at[0, g, b])
-
-    def forward(side, place, g, b):
+        return pltpu.make_async_copy(send.at[t, g, b], big.at[g, 2 + b], recv_sem.at[g, b])
+
+    def forward(side, slot, b):
         return pltpu.make_async_remote_copy(
-            src_ref=big.at[place, g, 2 + b],
-            dst_ref=big.at[place, g, 4 * side + b],
-            send_sem=fsend_sem.at[side, place, g, b],
-            recv_sem=frecv_sem.at[side, place, g, b],
+            src_ref=big.at[slot, 2 + b],
+            dst_ref=big.at[slot, 4 * side + b],
+            send_sem=fsend_sem.at[side, slot, b],
+            recv_sem=frecv_sem.at[side, slot, b],
             device_id=(t, left if side else right),
             device_id_type=MESH,
         )
@@ -171,28 +177,22 @@
 
         lax.fori_loop(0, 2, block, 0)
 
-    def places(pair):
-        return (2 * pair, 2 * pair + 1)
-
-    def send_unit(unit):
-        g = unit // PAIRS
-        for pair in range(PAIRS):
-            @pl.when(unit % PAIRS == pair)
-            def _():
-                for b in range(2):
-                    for place in places(pair):
-                        if place:
-                            run_copy(place, g, b).start()
+    def send_slot(slot):
+        for b in range(2):
+            run_copy(slot, b).start()
+
+    def send_nearest(g):
+        for b in range(2):
+            own_copy(g, b).start()
+        for i in range(2):
+            send_slot(GROUPS + 2 * g + i)
 
     for load in loads[:3]:
         load.wait()
     both_blocks(0)
     pl.semaphore_wait(barrier, RUNS + 1)
     halo.start()
-    for unit in range(AHEAD):
-        send_unit(jnp.int32(unit))
-    for b in range(2):
-        own_copy(0, b).start()
+    send_nearest(jnp.int32(0))
     loads[3].wait()
     loads[4].wait()
 
@@ -206,11 +206,16 @@
                 xh[:, pl.ds(samples, HALF)] = jnp.zeros((2 * CB, HALF), jnp.bfloat16)
 
         both_blocks(g)
-        for b in range(2):
-            own_copy(g, b).start()
+        send_nearest(g)
         return carry
 
     lax.fori_loop(1, GROUPS, later_group, 0)
+
+    def send_more(slot, carry):
+        send_slot(slot)
+        return carry
+
+    lax.fori_loop(3 * GROUPS, AHEAD, send_more, 0)
 
     base = edges[0, 0]
     bin_ids = lane % BINS
@@ -219,36 +224,25 @@
         masks[k] = inside.astype(jnp.float32).astype(jnp.bfloat16)
     acc[...] = jnp.zeros_like(acc)
 
-    def receive(unit):
-        g = unit // PAIRS
-        for pair in range(PAIRS):
-            @pl.when(unit % PAIRS == pair)
-            def _():
-                for b in range(2):
-                    for place in places(pair):
-                        if place == 0:
-                            own_copy(g, b).wait()
-                        else:
-                            run_copy(place, g, b).wait_recv()
-                        forward(0, place, g, b).start()
-                        forward(1, place, g, b).start()
-
-        @pl.when(unit + AHEAD < UNITS)
-        def _():
-            send_unit(unit + AHEAD)
-
-    def wait_neighbours(unit):
-        g = unit // PAIRS
-        first = 2 * (unit % PAIRS)
-        for b in range(2):
-            for i in range(2):
+    def receive(slot):
+        for b in range(2):
+            run_copy(slot, b).wait_recv()
+            forward(0, slot, b).start()
+            forward(1, slot, b).start()
+
+    def receive_own(g):
+        for b in range(2):
+            own_copy(g, b).wait()
+            forward(0, g, b).start()
+            forward(1, g, b).start()
+
+    def wait_neighbours(first, depth):
+        for b in range(2):
+            for i in range(depth):
                 for side in range(2):
-                    forward(side, first + i, g, b).wait_recv()
-
-    def multiply(unit, count, place_of):
-        g = unit // PAIRS
-        first = 2 * (unit % PAIRS)
-
+                    forward(side, first + i, b).wait_recv()
+
+    def multiply(first, depth, count, place_of):
         def one_left(item, carry):
             i = place_of(item)
             side = i // 4
@@ -257,7 +251,7 @@
             rights = jnp.concatenate(
                 [
                     jnp.concatenate(
-                        [big[first + p, g, base_right + n, q] for p in range(2) for q in range(2)],
+                        [big[first + p, base_right + n, q] for p in range(depth) for q in range(2)],
                         axis=1,
                     )
                     for n in range(2)
@@ -268,9 +262,9 @@
                 mask = masks[k]
                 pieces_re = []
                 pieces_im = []
-                for p in range(2):
-                    l0 = big[first + p, g, block, 0] * mask
-                    l1 = big[first + p, g, block, 1] * mask
+                for p in range(depth):
+                    l0 = big[first + p, block, 0] * mask
+                    l1 = big[first + p, block, 1] * mask
                     pieces_re += [l0, l1]
                     pieces_im += [l1, -l0]
                 both = jnp.concatenate(
@@ -286,47 +280,66 @@
 
         lax.fori_loop(0, count, one_left, 0)
 
-    def multiply_own(unit):
-        multiply(unit, 2, lambda item: item + 2)
-
-    def multiply_neighbours(unit):
-        wait_neighbours(unit)
-        multiply(unit, 4, lambda item: item + 2 * (item // 2))
-
-    def drain(unit):
-        g = unit // PAIRS
-        for pair in range(PAIRS):
-            @pl.when(unit % PAIRS == pair)
+    def multiply_own(first, depth):
+        multiply(first, depth, 2, lambda item: item + 2)
+
+    def multiply_neighbours(first, depth):
+        wait_neighbours(first, depth)
+        multiply(first, depth, 4, lambda item: item + 2 * (item // 2))
+
+    def drain(slot, carry):
+        for b in range(2):
+            @pl.when(slot >= GROUPS)
             def _():
-                for place in places(pair):
-                    for b in range(2):
-                        if place:
-                            run_copy(place, g, b).wait_send()
-                        forward(0, place, g, b).wait_send()
-                        forward(1, place, g, b).wait_send()
-
-    def steps(unit, carry):
-        receive(unit)
-        multiply_own(unit)
+                run_copy(slot, b).wait_send()
+
+            forward(0, slot, b).wait_send()
+            forward(1, slot, b).wait_send()
+        return carry
+
+    def paired_step(unit, carry):
+        first = 2 * unit
+        for i in range(2):
+            @pl.when(unit < GROUPS // 2)
+            def _():
+                receive_own(first + i)
+
+            @pl.when(unit >= GROUPS // 2)
+            def _():
+                receive(first + i)
+
+        @pl.when(first + AHEAD < SLOTS)
+        def _():
+            for i in range(2):
+                send_slot(first + AHEAD + i)
+
+        multiply_own(first, 2)
 
         @pl.when(unit >= 1)
         def _():
-            multiply_neighbours(unit - 1)
-
-        @pl.when(unit >= LATER)
+            multiply_neighbours(first - 2, 2)
+
+        @pl.when(first >= LATER)
         def _():
-            drain(unit - LATER)
-
-        return carry
-
-    lax.fori_loop(0, UNITS, steps, 0)
-    multiply_neighbours(UNITS - 1)
-
-    def drain_last(unit, carry):
-        drain(unit)
-        return carry
-
-    lax.fori_loop(UNITS - LATER, UNITS, drain_last, 0)
+            for i in range(2):
+                drain(first - LATER + i, 0)
+
+        return carry
+
+    lax.fori_loop(0, PAIRED // 2, paired_step, 0)
+    receive(jnp.int32(PAIRED))
+    multiply_own(PAIRED, 1)
+    multiply_neighbours(PAIRED - 2, 2)
+
+    def far_step(slot, carry):
+        receive(slot)
+        multiply_own(slot, 1)
+        multiply_neighbours(slot - 1, 1)
+        return carry
+
+    lax.fori_loop(PAIRED + 1, SLOTS, far_step, 0)
+    multiply_neighbours(SLOTS - 1, 1)
+    lax.fori_loop(PAIRED - LATER, SLOTS, drain, 0)
 
 
 def rows_kernel(edges, slots, acc, out, stage, out_sem):
@@ -378,14 +391,14 @@
             pltpu.VMEM((NF, NF), bf16),
             pltpu.VMEM((JG * CB, 2 * NF), jnp.float32),
             pltpu.VMEM((RUNS, GROUPS, 2, 2, CB, LANES), bf16),
-            pltpu.VMEM((RUNS, GROUPS, 6, 2, CB, LANES), bf16),
+            pltpu.VMEM((SLOTS, 6, 2, CB, LANES), bf16),
             pltpu.VMEM((BANDS_DEV, CB, LANES), bf16),
             pltpu.SemaphoreType.DMA((5,)),
             pltpu.SemaphoreType.DMA((2,)),
-            pltpu.SemaphoreType.DMA((RUNS, GROUPS, 2)),
-            pltpu.SemaphoreType.DMA((RUNS, GROUPS, 2)),
-            pltpu.SemaphoreType.DMA((2, RUNS, GROUPS, 2)),
-            pltpu.SemaphoreType.DMA((2, RUNS, GROUPS, 2)),
+            pltpu.SemaphoreType.DMA((SLOTS, 2)),
+            pltpu.SemaphoreType.DMA((SLOTS, 2)),
+            pltpu.SemaphoreType.DMA((2, SLOTS, 2)),
+            pltpu.SemaphoreType.DMA((2, SLOTS, 2)),
         ],
         compiler_params=pltpu.CompilerParams(
             collective_id=0, has_side_effects=True, vmem_limit_bytes=56 * 2**20

time: 119 us -> 119 us (level)
  the two profiles are of different devices: /device:TPU:25 before, /device:TPU:32 now
where the time goes in v3:
time: 119 us
  Pallas kernels  119 us (100%)
    pallas_call x1, Pallas kernels, shards(): pl.pallas_call(cross_kernel, out_shape=pltpu.VMEM(sums_shape, jnp.float32...  116 us
    pallas_call x1, Pallas kernels, shards(): pl.pallas_call(rows_kernel, out_shape=jax.ShapeDtypeStruct((ROWS, BANDS_D...  3.04 us

profile of v3, /device:TPU:32, one launch (start us, length us, event | category | flops | bytes accessed | tf_op | source)
XLA Modules:
  0.0 119.3 jit_solution(918408326411519190)
XLA Ops:
  0.0 0.0 copy-start.1
  0.0 0.0 copy-start
  0.0 116.3 %cross_spectra.1.acc = f32[12,4,2,128,128]{4,3,2,1,0:T(8,128)S(1)} custom-call(s32[2,4]{1,0:T(2,128)} %bitcast.2, bf16[256,4096]{1,0:T(8,128)(2,1)} %traces.1, bf16[512,512]{1,0:T(8,128)(2,1)} %constant.4.clone.tables, bf16[256,256]{1,0:T(8,128)(2,1)} %constant.5.clone.near), custom_call_target="tpu_custom_call" | custom-call | tf_op jit(solution)/shard_map/cross_spectra/pallas_call | solution.py:382
  116.3 0.0 copy-done.1
  116.3 0.0 copy-done
  116.3 3.0 %output_rows.1 = f32[10,4,2,128,128]{4,3,2,1,0:T(8,128)} custom-call(s32[2,4]{1,0:T(2,128)S(1)} %bitcast.3, s32[2,10]{1,0:T(2,128)S(1)} %bitcast.4, f32[12,4,2,128,128]{4,3,2,1,0:T(8,128)S(1)} %cross_spectra.1.acc), custom_call_target="tpu_custom_call" | custom-call | tf_op jit(solution)/shard_map/output_rows/pallas_call | solution.py:409
Async XLA Ops:
  0.0 116.3 %copy-start.1 = (s32[10,2]{0,1:T(2,128)S(1)}, s32[10,2]{0,1:T(2,128)}, u32[]{:S(2)}) copy-start(s32[10,2]{0,1:T(2,128)} %param.7) | copy-start | bytes 244
  0.0 116.3 %copy-start = (s32[4,2]{0,1:T(2,128)S(1)}, s32[4,2]{0,1:T(2,128)}, u32[]{:S(2)}) copy-start(s32[4,2]{0,1:T(2,128)} %param.6) | copy-start | bytes 100

commit v4 on v3

--- a/solution.py
+++ b/solution.py
@@ -22,7 +22,9 @@
 ROWS = 10
 SLOTS = RUNS * GROUPS
 PAIRED = SLOTS - GROUPS
-AHEAD = 16
+FOURS = 5 * GROUPS
+THREES = 6 * GROUPS
+AHEAD = 10
 LATER = 6
 
 whiten_eps = 1e-06
@@ -55,11 +57,18 @@
     early = (JG + 1) * HALF
 
     loads = [
-        pltpu.make_async_copy(tables, tab, load_sem.at[0]),
         pltpu.make_async_copy(
-            traces.at[:, pl.ds(0, early)], xh.at[:, pl.ds(0, early)], load_sem.at[1]
+            traces.at[pl.ds(0, CB), pl.ds(0, early)],
+            xh.at[pl.ds(0, CB), pl.ds(0, early)],
+            load_sem.at[0],
         ),
+        pltpu.make_async_copy(tables, tab, load_sem.at[1]),
         pltpu.make_async_copy(near, ban, load_sem.at[2]),
+        pltpu.make_async_copy(
+            traces.at[pl.ds(CB, CB), pl.ds(0, early)],
+            xh.at[pl.ds(CB, CB), pl.ds(0, early)],
+            load_sem.at[5],
+        ),
         pltpu.make_async_copy(
             traces.at[:, pl.ds(early, samples - early)],
             xh.at[:, pl.ds(early, samples - early)],
@@ -67,7 +76,7 @@
         ),
         pltpu.make_async_copy(edges_hbm, edges, load_sem.at[4]),
     ]
-    for load in loads:
+    for load in loads[:4]:
         load.start()
 
     def tm_at(step):
@@ -92,11 +101,14 @@
     )
 
     def route(slot):
-        near = (slot - GROUPS) // RUNS + 1
         place = (slot - GROUPS) % RUNS
-        far = slot // PAIRED
+        late = slot // THREES
+        fours = slot // FOURS - late
+        early = 1 - late - fours
+        near = early * ((slot - GROUPS) // RUNS + 1) + 4 * fours + 3 * late
         hop = near + (slot % 2) * (RUNS - 2 * near)
-        return tm_at(hop), far * place + (1 - far) * (place // 2)
+        g = early * (place // 2) + fours * (slot - FOURS) + late * ((slot - THREES) // 2)
+        return tm_at(hop), g
 
     def run_copy(slot, b):
         run, g = route(slot)
@@ -170,31 +182,28 @@
                 for s, tile in enumerate((u0, u1, u2, u3)):
                     send[h * 4 + s, g, b, q] = tile.astype(jnp.bfloat16)
 
-    def both_blocks(g):
-        def block(b, carry):
-            transform(g, b)
-            return carry
-
-        lax.fori_loop(0, 2, block, 0)
-
     def send_slot(slot):
         for b in range(2):
             run_copy(slot, b).start()
 
-    def send_nearest(g):
-        for b in range(2):
-            own_copy(g, b).start()
+    def send_nearest(g, b):
         for i in range(2):
-            send_slot(GROUPS + 2 * g + i)
+            run_copy(GROUPS + 2 * g + i, b).start()
+        own_copy(g, b).start()
 
     for load in loads[:3]:
         load.wait()
-    both_blocks(0)
+    transform(jnp.int32(0), jnp.int32(0))
+    for load in loads[4:]:
+        load.start()
     pl.semaphore_wait(barrier, RUNS + 1)
+    send_nearest(jnp.int32(0), 0)
     halo.start()
-    send_nearest(jnp.int32(0))
     loads[3].wait()
-    loads[4].wait()
+    transform(jnp.int32(0), jnp.int32(1))
+    send_nearest(jnp.int32(0), 1)
+    for load in loads[4:]:
+        load.wait()
 
     def later_group(g, carry):
         @pl.when(g == GROUPS - 1)
@@ -205,8 +214,12 @@
             def _():
                 xh[:, pl.ds(samples, HALF)] = jnp.zeros((2 * CB, HALF), jnp.bfloat16)
 
-        both_blocks(g)
-        send_nearest(g)
+        def block(b, inner):
+            transform(g, b)
+            send_nearest(g, b)
+            return inner
+
+        lax.fori_loop(0, 2, block, 0)
         return carry
 
     lax.fori_loop(1, GROUPS, later_group, 0)
@@ -215,7 +228,7 @@
         send_slot(slot)
         return carry
 
-    lax.fori_loop(3 * GROUPS, AHEAD, send_more, 0)
+    lax.fori_loop(3 * GROUPS, GROUPS + AHEAD, send_more, 0)
 
     base = edges[0, 0]
     bin_ids = lane % BINS
@@ -308,7 +321,7 @@
             def _():
                 receive(first + i)
 
-        @pl.when(first + AHEAD < SLOTS)
+        @pl.when((first >= GROUPS) & (first + AHEAD < SLOTS))
         def _():
             for i in range(2):
                 send_slot(first + AHEAD + i)
@@ -393,7 +406,7 @@
             pltpu.VMEM((RUNS, GROUPS, 2, 2, CB, LANES), bf16),
             pltpu.VMEM((SLOTS, 6, 2, CB, LANES), bf16),
             pltpu.VMEM((BANDS_DEV, CB, LANES), bf16),
-            pltpu.SemaphoreType.DMA((5,)),
+            pltpu.SemaphoreType.DMA((6,)),
             pltpu.SemaphoreType.DMA((2,)),
             pltpu.SemaphoreType.DMA((SLOTS, 2)),
             pltpu.SemaphoreType.DMA((SLOTS, 2)),

time: 119 us -> 116 us (0.975)
  the two profiles are of different devices: /device:TPU:32 before, /device:TPU:25 now
where the time goes in v4:
time: 116 us; the launch traced here: 115 us
  Pallas kernels  115 us (99%)
    pallas_call x1, Pallas kernels, shards(): pl.pallas_call(cross_kernel, out_shape=pltpu.VMEM(sums_shape, jnp.float32...  112 us
    pallas_call x1, Pallas kernels, shards(): pl.pallas_call(rows_kernel, out_shape=jax.ShapeDtypeStruct((ROWS, BANDS_D...  3.04 us

profile of v4, /device:TPU:25, one launch (start us, length us, event | category | flops | bytes accessed | tf_op | source)
XLA Modules:
  0.0 115.1 jit_solution(607434270019359337)
XLA Ops:
  0.0 0.0 copy-start.1
  0.0 0.0 copy-start
  0.0 112.1 %cross_spectra.1.acc = f32[12,4,2,128,128]{4,3,2,1,0:T(8,128)S(1)} custom-call(s32[2,4]{1,0:T(2,128)} %bitcast.2, bf16[256,4096]{1,0:T(8,128)(2,1)} %traces.1, bf16[512,512]{1,0:T(8,128)(2,1)} %constant.4.clone.tables, bf16[256,256]{1,0:T(8,128)(2,1)} %constant.5.clone.near), custom_call_target="tpu_custom_call" | custom-call | tf_op jit(solution)/shard_map/cross_spectra/pallas_call | solution.py:395
  112.1 0.0 copy-done.1
  112.1 0.0 copy-done
  112.1 3.0 %output_rows.1 = f32[10,4,2,128,128]{4,3,2,1,0:T(8,128)} custom-call(s32[2,4]{1,0:T(2,128)S(1)} %bitcast.3, s32[2,10]{1,0:T(2,128)S(1)} %bitcast.4, f32[12,4,2,128,128]{4,3,2,1,0:T(8,128)S(1)} %cross_spectra.1.acc), custom_call_target="tpu_custom_call" | custom-call | tf_op jit(solution)/shard_map/output_rows/pallas_call | solution.py:422
Async XLA Ops:
  0.0 112.1 %copy-start.1 = (s32[10,2]{0,1:T(2,128)S(1)}, s32[10,2]{0,1:T(2,128)}, u32[]{:S(2)}) copy-start(s32[10,2]{0,1:T(2,128)} %param.7) | copy-start | bytes 244
  0.0 112.1 %copy-start = (s32[4,2]{0,1:T(2,128)S(1)}, s32[4,2]{0,1:T(2,128)}, u32[]{:S(2)}) copy-start(s32[4,2]{0,1:T(2,128)} %param.6) | copy-start | bytes 100

commit v5 on v4

--- a/solution.py
+++ b/solution.py
@@ -55,6 +55,18 @@
     chans = 32
     samples = 4096
     early = (JG + 1) * HALF
+
+    def tm_at(step):
+        return lax.rem(t + step, RUNS)
+
+    right = lax.rem(ch + 1, chans)
+    left = lax.rem(ch + chans - 1, chans)
+
+    barrier = pltpu.get_barrier_semaphore()
+    for hop in range(1, RUNS):
+        pl.semaphore_signal(barrier, inc=1, device_id=(tm_at(hop), ch), device_id_type=MESH)
+    pl.semaphore_signal(barrier, inc=1, device_id=(t, right), device_id_type=MESH)
+    pl.semaphore_signal(barrier, inc=1, device_id=(t, left), device_id_type=MESH)
 
     loads = [
         pltpu.make_async_copy(
@@ -78,18 +90,6 @@
     ]
     for load in loads[:4]:
         load.start()
-
-    def tm_at(step):
-        return lax.rem(t + step, RUNS)
-
-    right = lax.rem(ch + 1, chans)
-    left = lax.rem(ch + chans - 1, chans)
-
-    barrier = pltpu.get_barrier_semaphore()
-    for hop in range(1, RUNS):
-        pl.semaphore_signal(barrier, inc=1, device_id=(tm_at(hop), ch), device_id_type=MESH)
-    pl.semaphore_signal(barrier, inc=1, device_id=(t, right), device_id_type=MESH)
-    pl.semaphore_signal(barrier, inc=1, device_id=(t, left), device_id_type=MESH)
 
     halo = pltpu.make_async_remote_copy(
         src_ref=traces.at[:, pl.ds(0, HALF)],

time: 116 us -> 116 us (level)
  no operation moved by 1% of the time
where the time goes in v5:
time: 116 us; the launch traced here: 115 us
  Pallas kernels  115 us (99%)
    pallas_call x1, Pallas kernels, shards(): pl.pallas_call(cross_kernel, out_shape=pltpu.VMEM(sums_shape, jnp.float32...  112 us
    pallas_call x1, Pallas kernels, shards(): pl.pallas_call(rows_kernel, out_shape=jax.ShapeDtypeStruct((ROWS, BANDS_D...  3.04 us

profile of v5, /device:TPU:25, one launch (start us, length us, event | category | flops | bytes accessed | tf_op | source)
XLA Modules:
  0.0 115.2 jit_solution(9610983103344166793)
XLA Ops:
  0.0 0.0 copy-start.1
  0.0 0.0 copy-start
  0.0 112.1 %cross_spectra.1.acc = f32[12,4,2,128,128]{4,3,2,1,0:T(8,128)S(1)} custom-call(s32[2,4]{1,0:T(2,128)} %bitcast.2, bf16[256,4096]{1,0:T(8,128)(2,1)} %traces.1, bf16[512,512]{1,0:T(8,128)(2,1)} %constant.4.clone.tables, bf16[256,256]{1,0:T(8,128)(2,1)} %constant.5.clone.near), custom_call_target="tpu_custom_call" | custom-call | tf_op jit(solution)/shard_map/cross_spectra/pallas_call | solution.py:395
  112.1 0.0 copy-done.1
  112.1 0.0 copy-done
  112.2 3.0 %output_rows.1 = f32[10,4,2,128,128]{4,3,2,1,0:T(8,128)} custom-call(s32[2,4]{1,0:T(2,128)S(1)} %bitcast.3, s32[2,10]{1,0:T(2,128)S(1)} %bitcast.4, f32[12,4,2,128,128]{4,3,2,1,0:T(8,128)S(1)} %cross_spectra.1.acc), custom_call_target="tpu_custom_call" | custom-call | tf_op jit(solution)/shard_map/output_rows/pallas_call | solution.py:422
Async XLA Ops:
  0.0 112.1 %copy-start.1 = (s32[10,2]{0,1:T(2,128)S(1)}, s32[10,2]{0,1:T(2,128)}, u32[]{:S(2)}) copy-start(s32[10,2]{0,1:T(2,128)} %param.7) | copy-start | bytes 244
  0.0 112.1 %copy-start = (s32[4,2]{0,1:T(2,128)S(1)}, s32[4,2]{0,1:T(2,128)}, u32[]{:S(2)}) copy-start(s32[4,2]{0,1:T(2,128)} %param.6) | copy-start | bytes 100
